TPU v7x, 512 devices: a whole 4x4x16 slice. The times are simulated.
512 devices in a mesh: dp: 16 (over x, z_lo), sp: 32 (over z_hi, y, core).
Axes of the slice: x: 4, y: 4, z: 16 (z_hi: 4, z_lo: 4; z = z_hi * 4 + z_lo), core: 2. Of those that a mesh axis runs over, the one named last changes fastest.
Arguments:
- hidden: bfloat16 [16, 4096, 2048], P('dp', 'sp'), may hold values from -6 to 6
- queries: bfloat16 [16, 4096, 2048], P('dp', 'sp'), may hold values from -160 to 160
- key_states: bfloat16 [16, 4096, 512], P('dp', 'sp'), may hold values from -4 to 4
- upstream: bfloat16 [16, 4096, 2048], P('dp', 'sp'), may hold values from -6 to 6
- value_weight: bfloat16 [2048, 512], P('dp'), may hold values from -0.125 to 0.125
- doc_ids: int32 [16, 4096], P('dp', 'sp'), may hold values from 0 to 7, never falling along the last dimension, each value on 1 to 2048 neighbouring positions
Outputs:
- attn_out: bfloat16 [16, 4096, 2048], P('dp', 'sp')
- grad_hidden: bfloat16 [16, 4096, 2048], P('dp', 'sp')
- grad_weight: float32 [2048, 512], P(('dp', 'sp'))
Inputs may be any that keep to these rules, and one draw needn't show every extreme that they name: `doc_ids`: never falling along a sequence; each document has 1 to 2048 positions, one exactly 2048.
All inputs are finite; a program needn't handle non-finite values.
Results may differ from a plain program's by a relative error of at most 0.015.
Values may be sent and summed in bfloat16 or wider, within the bound.
No kernel may reach another device: no remote copies, remote signals or barrier semaphores. Data moves between devices by JAX's collectives and lax.ppermute only.
A program may use at most 64 MiB of HBM per device.

v0:
```python
import jax
import jax.numpy as jnp
from jax import lax
from jax.sharding import PartitionSpec as P

D = 2048
H = 32
KVH = 8
HD = 64


def attend(head_query, head_keyval, documents):
    seq_len = head_query.shape[0]
    block_rows = min(512, seq_len)
    block_count = seq_len // block_rows
    query_part = head_query[:, :HD]
    cotangent_part = head_query[:, HD:]
    key_part = head_keyval[:, :HD]
    value_part = head_keyval[:, HD:]
    positions = jnp.arange(seq_len, dtype=jnp.int32)

    def step(block_index, state_pair):
        outputs, gradient = state_pair
        first_row = block_index * block_rows
        query_block = lax.dynamic_slice_in_dim(query_part, first_row, block_rows, 0)
        cotangent_block = lax.dynamic_slice_in_dim(cotangent_part, first_row, block_rows, 0)
        block_docs = lax.dynamic_slice_in_dim(documents, first_row, block_rows, 0)
        block_positions = first_row + jnp.arange(block_rows, dtype=jnp.int32)
        score = lax.dot_general(
            query_block, key_part, (((1,), (1,)), ((), ())), preferred_element_type=jnp.float32
        ) * (1.0 / HD**0.5)
        allowed = (block_docs[:, None] == documents[None, :]) & (
            positions[None, :] <= block_positions[:, None]
        )
        score = jnp.where(allowed, score, jnp.float32(-1e30))
        row_max = jnp.max(score, axis=1, keepdims=True)
        raised = jnp.exp(score - row_max)
        weights_bf = (raised / jnp.sum(raised, axis=1, keepdims=True)).astype(jnp.bfloat16)
        block_out = jnp.dot(weights_bf, value_part, preferred_element_type=jnp.float32).astype(
            jnp.bfloat16
        )
        outputs = lax.dynamic_update_slice_in_dim(outputs, block_out, first_row, 0)
        gradient = gradient + lax.dot_general(
            weights_bf,
            cotangent_block,
            (((0,), (0,)), ((), ())),
            preferred_element_type=jnp.float32,
        )
        return (outputs, gradient)

    start_pair = (jnp.zeros((seq_len, HD), jnp.bfloat16), jnp.zeros((seq_len, HD), jnp.float32))
    outputs, gradient = lax.fori_loop(0, block_count, step, start_pair)
    return jnp.concatenate([outputs, gradient.astype(jnp.bfloat16)], axis=1)


def body(hidden, queries, key_states, upstream, value_weight, doc_ids):
    tokens = hidden.shape[1]
    groups = H // KVH
    hidden_rows = hidden[0]
    full_weight = lax.all_gather(value_weight, "dp", axis=0, tiled=True)
    value = jnp.dot(hidden_rows, full_weight, preferred_element_type=jnp.float32).astype(
        jnp.bfloat16
    )
    keyed = jnp.repeat(key_states[0].reshape(tokens, KVH, HD), groups, axis=1)
    valued = jnp.repeat(value.reshape(tokens, KVH, HD), groups, axis=1)
    paired_kv = jnp.concatenate([keyed, valued], axis=2)
    paired_q = jnp.concatenate(
        [queries[0].reshape(tokens, H, HD), upstream[0].reshape(tokens, H, HD)], axis=2
    )
    head_q, head_kv = (
        lax.all_to_all(paired_q, "sp", split_axis=1, concat_axis=0, tiled=True),
        lax.all_to_all(paired_kv, "sp", split_axis=1, concat_axis=0, tiled=True),
    )
    documents = lax.all_gather(doc_ids[0], "sp", axis=0, tiled=True)
    results = jax.vmap(attend, in_axes=(1, 1, None), out_axes=1)(head_q, head_kv, documents)
    returned = lax.all_to_all(results, "sp", split_axis=0, concat_axis=1, tiled=True)
    attn_out = returned[:, :, :HD].reshape(1, tokens, H * HD)
    value_grad = (
        returned[:, :, HD:].astype(jnp.float32).reshape(tokens, KVH, groups, HD).sum(axis=2)
    )
    value_grad = value_grad.astype(jnp.bfloat16).reshape(tokens, KVH * HD)
    grad_rows = lax.dot_general(
        value_grad, full_weight, (((1,), (1,)), ((), ())), preferred_element_type=jnp.float32
    )
    grad_hidden = grad_rows.astype(jnp.bfloat16).reshape(1, tokens, D)
    grad_weight = lax.psum_scatter(
        lax.dot_general(
            hidden_rows, value_grad, (((0,), (0,)), ((), ())), preferred_element_type=jnp.float32
        ),
        ("dp", "sp"),
        scatter_dimension=0,
        tiled=True,
    )
    return (attn_out, grad_hidden, grad_weight)


def solution(mesh):
    return jax.shard_map(
        body,
        mesh=mesh,
        in_specs=(
            P("dp", "sp", None),
            P("dp", "sp", None),
            P("dp", "sp", None),
            P("dp", "sp", None),
            P("dp", None),
            P("dp", "sp"),
        ),
        out_specs=(P("dp", "sp", None), P("dp", "sp", None), P(("dp", "sp"), None)),
        check_vma=False,
    )
```

profile of v0, /device:TPU:2, one launch (start us, length us, event | category | flops | bytes accessed | tf_op | source)
XLA Modules:
  0.0 939.3 jit_solution(17589983539403111429)
XLA Ops:
  11.7 18.1 %all-to-all-start = ((bf16[128,32,128]{0,2,1:T(8,128)(2,1)}), bf16[128,32,128]{0,2,1:T(8,128)(2,1)S(1)}, u32[]{:S(2)}, u32[]{:S(2)}) async-start(bf16[128,32,128]{0,2,1:T(8,128)(2,1)} %pad_maximum_fusion), calls=%async_computation | async-start | bytes 2097152 | tf_op jit(solution)/shard_map/all_to_all | solution.py:71
  30.1 100.5 %all-gather.3.cloned.1.call-done = bf16[2048,512]{1,0:T(8,128)(2,1)} async-done(((bf16[128,512]{1,0:T(8,128)(2,1)}), bf16[2048,512]{1,0:T(8,128)(2,1)}) %all-gather.3.cloned.1.call-update) | async-done | bytes 2097168 | tf_op jit(solution)/shard_map/all_gather | solution.py:60
  130.6 2.0 convolution_convert_fusion.2
  133.5 1.6 pad_maximum_fusion.1
  135.1 14.0 %all-to-all-start.1 = ((bf16[128,32,128]{2,0,1:T(8,128)(2,1)}), bf16[128,32,128]{2,0,1:T(8,128)(2,1)S(1)}, u32[]{:S(2)}, u32[]{:S(2)}) async-start(bf16[128,32,128]{2,0,1:T(8,128)(2,1)} %pad_maximum_fusion.1), calls=%async_computation.1 | async-start | bytes 2097152 | tf_op jit(solution)/shard_map/all_to_all | solution.py:72
  149.1 89.8 %all-gather = s32[1,4096]{1,0:T(1,128)S(1)} all-gather(s32[1,128]{1,0:T(1,128)S(1)} %copy-done.7), channel_id=2, replica_groups=mesh['dp'=16,'sp'=32] {'sp'}, dimensions={1}, use_global_device_ids=true | all-gather | bytes 16896 | tf_op jit(solution)/shard_map/all_gather | solution.py:74
  238.9 2.3 copy.64
  241.2 3.2 slice_bitcast_fusion
  245.5 2.9 slice_bitcast_fusion.1
  248.5 123.3 %while.19 = (s32[]{:T(128)}, bf16[1,4096,64]{1,2,0:T(8,128)(2,1)S(1)}, f32[1,4096,64]{1,2,0:T(8,128)S(1)}, s32[4096]{0:T(1024)S(1)}, bf16[1,4096,64]{2,1,0:T(8,1...) while((s32[]{:T(128)}, ...), condition=%wide.region_4.5_spmd.clone, body=%wide.region_0.4_spmd.clone.sunk | while | flops 828964352 | bytes 58757428 | solution.py:52
  248.7 3.7 fusion.40
  253.6 3.3 divide_convert_fusion.2
  256.9 3.4 fusion.43
  261.1 2.1 fusion.42
  264.1 3.7 fusion.40
  269.1 3.3 divide_convert_fusion.2
  272.4 3.4 fusion.43
  276.6 2.1 fusion.42
  279.5 3.7 fusion.40
  284.5 3.3 divide_convert_fusion.2
  287.8 3.4 fusion.43
  292.0 2.1 fusion.42
  295.0 3.7 fusion.40
  300.0 3.3 divide_convert_fusion.2
  303.3 3.4 fusion.43
  307.4 2.1 fusion.42
  310.4 3.7 fusion.40
  315.4 3.3 divide_convert_fusion.2
  318.7 3.4 fusion.43
  322.9 2.1 fusion.42
  325.9 3.7 fusion.40
  330.9 3.3 divide_convert_fusion.2
  334.2 3.4 fusion.43
  338.3 2.1 fusion.42
  341.3 3.7 fusion.40
  346.3 3.3 divide_convert_fusion.2
  349.6 3.4 fusion.43
  353.8 2.1 fusion.42
  356.8 3.7 fusion.40
  361.7 3.3 divide_convert_fusion.2
  365.0 3.4 fusion.43
  369.2 2.1 fusion.42
  374.8 63.5 %all_to_all.54 = bf16[32,2,8192]{2,1,0:T(2,128)(2,1)S(1)} all-to-all(bf16[32,2,8192]{2,1,0:T(2,128)(2,1)S(1)} %reshape.233), channel_id=1, replica_groups=mesh['dp'=16,'sp'=32] {'sp'}, dimensions={0} | all-to-all | bytes 2097152 | tf_op jit(solution)/shard_map/all_to_all | solution.py:76
  438.4 3.4 reshape.234
  441.8 1.7 copy.79
  444.1 2.7 convolution_bitcast_fusion.1
  448.1 3.2 fusion.16
  451.4 479.3 %all-reduce.3.cloned.1.call-done = f32[2048,512]{0,1:T(8,128)} async-done(((f32[2048,512]{0,1:T(8,128)}), f32[2048,512]{0,1:T(8,128)}) %all-reduce.3.cloned.1.call-update) | async-done | bytes 4194320
  (115 shorter events, 36.8 us)
Async XLA Ops:
  7.2 123.5 %copy-start = (bf16[1,128,2048]{2,1,0:T(8,128)(2,1)S(1)}, bf16[1,128,2048]{2,1,0:T(8,128)(2,1)}, u32[]{:S(2)}) copy-start(bf16[1,128,2048]{2,1,0:T(8,128)(2,1)} %param.10) | copy-start | bytes 1572868
  7.2 22.6 %copy-start.4 = (bf16[1,128,512]{2,1,0:T(8,128)(2,1)S(1)}, bf16[1,128,512]{2,1,0:T(8,128)(2,1)}, u32[]{:S(2)}) copy-start(bf16[1,128,512]{2,1,0:T(8,128)(2,1)} %param.12) | copy-start | bytes 393220
  7.2 123.4 %all-gather.3.cloned.1.call-start = ((), (), s32[]{:S(2)}) async-start(), calls=%async_computation.3 | async-start | bytes 2228224 | tf_op jit(solution)/shard_map/all_gather | solution.py:60
  11.7 123.4 %all-to-all-start = ((bf16[128,32,128]{0,2,1:T(8,128)(2,1)}), bf16[128,32,128]{0,2,1:T(8,128)(2,1)S(1)}, u32[]{:S(2)}, u32[]{:S(2)}) async-start(bf16[128,32,128]{0,2,1:T(8,128)(2,1)} %pad_maximum_fusion), calls=%async_computation | async-start | bytes 2097152 | tf_op jit(solution)/shard_map/all_to_all | solution.py:71
  132.8 16.3 %copy-start.7 = (s32[1,128]{1,0:T(1,128)S(1)}, s32[1,128]{1,0:T(1,128)}, u32[]{:S(2)}) copy-start(s32[1,128]{1,0:T(1,128)} %param.15) | copy-start | bytes 1540
  135.1 14.0 %copy-start.3 = (bf16[128,32,128]{0,2,1:T(8,128)(2,1)}, bf16[128,32,128]{0,2,1:T(8,128)(2,1)S(1)}, u32[]{:S(2)}) copy-start(bf16[128,32,128]{0,2,1:T(8,128)(2,1)S(1)} %all-to-all-done) | copy-start | bytes 3145732
  135.1 109.4 %all-to-all-start.1 = ((bf16[128,32,128]{2,0,1:T(8,128)(2,1)}), bf16[128,32,128]{2,0,1:T(8,128)(2,1)S(1)}, u32[]{:S(2)}, u32[]{:S(2)}) async-start(bf16[128,32,128]{2,0,1:T(8,128)(2,1)} %pad_maximum_fusion.1), calls=%async_computation.1 | async-start | bytes 2097152 | tf_op jit(solution)/shard_map/all_to_all | solution.py:72
  149.0 781.6 %all-reduce.3.cloned.1.call-start = ((), (), s32[]{:S(2)}) async-start(), calls=%async_computation.4 | async-start | bytes 8388608
  241.2 7.2 copy-start.5
  241.2 7.2 copy-start.6
  244.5 1.0 copy-start.2
  256.9 4.2 copy-start.1
  272.4 4.2 copy-start.1
  287.8 4.2 copy-start.1
  303.3 4.2 copy-start.1
  318.7 4.2 copy-start.1
  334.2 4.2 copy-start.1
  349.6 4.2 copy-start.1
  365.0 4.2 copy-start.1
Sparse Core Ops, SparseCore 0:
  10.1 120.4 all-gather.2
  446.9 483.7 all-reduce.2
where the time goes:
time: 940 us; the launch traced here: 939 us
  waiting for transfers between devices  581 us (62%)
  blocking collectives  153 us (16%)
  matrix products  81.2 us (9%)
  other arithmetic  48.2 us (5%)
  starting transfers between devices  32.2 us (3%)
  local copies, waits for them, and re-layouts  29.4 us (3%)
  between operations  14.3 us (2%)
    unnamed x3, waiting for transfers between devices  480 us
    all_gather x1, waiting for transfers between devices, body(): full_weight = lax.all_gather(value_weight, 'dp', axis=0, tiled=True)  101 us
    all_gather x1, blocking collectives, body(): documents = lax.all_gather(doc_ids[0], 'sp', axis=0, tiled=True)  89.8 us
    all_to_all x1, blocking collectives, body(): lax.all_to_all(results, 'sp', split_axis=0, concat_axis=1, tiled=True)  63.5 us
    dot_general x8, matrix products, step(): lax.dot_general(query_block, key_part, (((1,), (1,)), ((), ())), preferre...  29.6 us
    dot_general x8, matrix products, step(): lax.dot_general(weights_bf, cotangent_block, (((0,), (0,)), ((), ())), pr...  27 us
    convert_element_type x8, other arithmetic, step(): (raised / jnp.sum(raised, axis=1, keepdims=True)).astype(jnp.bfloat16)  26.3 us
  transfers between devices with their start and end apart: 4, of which 2 were waited for; matrix products, arithmetic and copies ran while one was open for 2% of the time, Pallas kernels for 0%

commit v1 on v0

v1 whole, which is shorter than its diff:
```python
import jax
import jax.numpy as jnp
import numpy as np
from jax import lax
from jax.experimental import pallas as pl
from jax.experimental.pallas import tpu as pltpu
from jax.sharding import Mesh, PartitionSpec as P

D = 2048
H = 32
KVH = 8
HD = 64
GROUPS = H // KVH
TOK = 128
NB = 8
KVD = KVH * HD
WIN = 3 * NB
LANES = GROUPS * TOK
BK = 256
DOCROWS = 16
NEG = -1e30
BF = jnp.bfloat16
F32 = jnp.float32
YC = ("y", "c")
VMEM = 56 * 1024 * 1024


def params(limit=VMEM):
    return pltpu.CompilerParams(vmem_limit_bytes=limit)


def dot(a, b, contract):
    return lax.dot_general(a, b, ((contract[0], contract[1]), ((), ())), preferred_element_type=F32)


def pack_keys_kernel(key_ref, doc_ref, out_ref):
    turned = key_ref[0].T
    docs = jnp.broadcast_to((doc_ref[...] + 1).astype(F32), (DOCROWS, TOK)).astype(BF)
    for g in range(KVH):
        out_ref[g, :HD, :] = turned[g * HD : (g + 1) * HD]
        out_ref[g, HD:, :] = docs


def pack_keys(key_states, doc_ids):
    return pl.pallas_call(
        pack_keys_kernel,
        out_shape=jax.ShapeDtypeStruct((KVH, HD + DOCROWS, TOK), BF),
        name="pack_keys",
        compiler_params=params(),
    )(key_states, doc_ids)


def pack_rows_kernel(query_ref, up_ref, hidden_ref, out_ref):
    part = GROUPS * HD
    row = lax.broadcasted_iota(jnp.int32, (TOK, TOK), 0)
    col = lax.broadcasted_iota(jnp.int32, (TOK, TOK), 1)
    wanted = ((row // 4) % 4) * 32 + (row // 16) * 4 + row % 4
    pick = (col == wanted).astype(F32).astype(BF)
    for g in range(KVH):
        cols = slice(g * part, (g + 1) * part)
        out_ref[g, :part, :] = (query_ref[0, :, cols] * BF(0.125)).T
        out_ref[g, part : 2 * part, :] = up_ref[0, :, cols].T
    for d in range(16):
        moved = dot(pick, hidden_ref[0, :, d * TOK : (d + 1) * TOK], ((1,), (1,))).astype(BF)
        for yc in range(8):
            out_ref[yc, 2 * part + d * 16 : 2 * part + (d + 1) * 16, :] = moved[yc * 16 : (yc + 1) * 16]


def pack_rows(queries, upstream, hidden):
    return pl.pallas_call(
        pack_rows_kernel,
        out_shape=jax.ShapeDtypeStruct((KVH, 3 * GROUPS * HD, TOK), BF),
        name="pack_rows",
        compiler_params=params(),
    )(queries, upstream, hidden)


def first_keys(key_refs):
    docs = [ref[:, HD : HD + 1, :].astype(F32).reshape(NB, TOK) for ref in key_refs]
    starts = []
    for d in range(8):
        total = jnp.zeros((NB, TOK), F32)
        for block in docs:
            total = total + jnp.where(block < d + 1, 1.0, 0.0)
        starts.append(jnp.sum(total))
    own = docs[-1]
    rows = jnp.full((NB, TOK), starts[0], F32)
    for d in range(1, 8):
        rows = jnp.where(own >= d + 1, starts[d], rows)
    return rows.astype(jnp.int32)


def load_keys(key_refs, keys_ref):
    for n, ref in enumerate(key_refs):
        for b in range(NB):
            at = (n * NB + b) * TOK
            keys_ref[at : at + TOK, :] = ref[b, :HD, :].T


def head_lanes(ref, block, offset):
    return jnp.concatenate([ref[block, offset + h * HD : offset + (h + 1) * HD, :] for h in range(GROUPS)], axis=1)


def ranges(start_ref, block):
    row = start_ref[pl.ds(block, 1), :]
    low = jnp.min(row)
    high = jnp.max(row)
    last = (2 * NB + block) // (BK // TOK)
    begin = low // BK
    plain = jnp.minimum((high + BK - 1) // BK, last)
    return jnp.concatenate([row] * GROUPS, axis=1), begin, plain, last


def masked(score, row, tile, block, causal):
    at = tile * BK + lax.broadcasted_iota(jnp.int32, score.shape, 0)
    keep = at >= row
    if causal:
        mine = (2 * NB + block) * TOK + (lax.broadcasted_iota(jnp.int32, score.shape, 1) & (TOK - 1))
        keep = keep & (at <= mine)
    return jnp.where(keep, score, NEG)


def fold(x, op):
    out = x[0:8]
    for i in range(1, x.shape[0] // 8):
        out = op(out, x[i * 8 : i * 8 + 8])
    return out


def grads_kernel(
    far_ref, near_ref, own_ref, rows_ref, out_far, out_near, out_own, lse_ref, keys_ref, start_ref, score_ref, prob_ref, grad_ref
):
    key_refs = (far_ref, near_ref, own_ref)
    load_keys(key_refs, keys_ref)
    start_ref[...] = first_keys(key_refs)
    grad_ref[...] = jnp.zeros_like(grad_ref)

    def one_block(block, _):
        row, begin, plain, last = ranges(start_ref, block)
        query = head_lanes(rows_ref, block, 0)

        def put(tile, high, mode):
            at = pl.multiple_of(tile * BK, BK)
            score = jnp.dot(keys_ref[pl.ds(at, BK), :], query, preferred_element_type=F32)
            if mode:
                score = masked(score, row, tile, block, mode == 2)
            score_ref[pl.ds(at, BK), :] = score
            return jnp.maximum(high, fold(score, jnp.maximum))

        high = jnp.full((8, LANES), NEG, F32)
        high = lax.fori_loop(begin, plain, lambda t, h: put(t, h, 1), high)
        high = lax.fori_loop(plain, last, lambda t, h: put(t, h, 0), high)
        high = put(last, high, 2)
        high = jnp.max(high, axis=0, keepdims=True)

        def raise_(tile, total):
            at = pl.multiple_of(tile * BK, BK)
            raised = jnp.exp(score_ref[pl.ds(at, BK), :] - high)
            prob_ref[pl.ds(at, BK), :] = raised.astype(BF)
            return total + fold(raised, jnp.add)

        total = lax.fori_loop(begin, last + 1, raise_, jnp.zeros((8, LANES), F32))
        total = jnp.sum(total, axis=0, keepdims=True)
        lse_ref[block] = jnp.broadcast_to(high + jnp.log(total), (8, LANES))
        up = (head_lanes(rows_ref, block, GROUPS * HD).astype(F32) * (1.0 / total)).astype(BF)

        def back(tile, _):
            at = pl.multiple_of(tile * BK, BK)
            grad_ref[pl.ds(at, BK), :] += dot(prob_ref[pl.ds(at, BK), :], up, ((1,), (1,)))
            return 0

        lax.fori_loop(begin, last + 1, back, 0)
        return 0

    lax.fori_loop(0, NB, one_block, 0)
    for n, out in enumerate((out_far, out_near, out_own)):
        for b in range(NB):
            at = (n * NB + b) * TOK
            out[b] = grad_ref[at : at + TOK, :].T.astype(out.dtype)


def grads(keys, rows):
    shape = (NB, HD, TOK)
    return pl.pallas_call(
        grads_kernel,
        out_shape=(
            jax.ShapeDtypeStruct(shape, BF),
            jax.ShapeDtypeStruct(shape, BF),
            jax.ShapeDtypeStruct(shape, F32),
            jax.ShapeDtypeStruct((NB, 8, LANES), F32),
        ),
        scratch_shapes=[
            pltpu.VMEM((WIN * TOK, HD), BF),
            pltpu.VMEM((NB, TOK), jnp.int32),
            pltpu.VMEM((WIN * TOK, LANES), F32),
            pltpu.VMEM((WIN * TOK, LANES), BF),
            pltpu.VMEM((WIN * TOK, HD), F32),
        ],
        name="grads",
        compiler_params=params(),
    )(*keys, rows)


def outs_kernel(
    far_ref, near_ref, own_ref, vfar_ref, vnear_ref, vown_ref, rows_ref, lse_ref, out_ref, keys_ref, start_ref, value_ref
):
    key_refs = (far_ref, near_ref, own_ref)
    load_keys(key_refs, keys_ref)
    start_ref[...] = first_keys(key_refs)
    per = BK // TOK
    for n, ref in enumerate((vfar_ref, vnear_ref, vown_ref)):
        for b in range(NB):
            value_ref[(n * NB + b) // per, :, (b % per) * TOK : (b % per + 1) * TOK] = ref[b]

    def one_block(block, _):
        row, begin, plain, last = ranges(start_ref, block)
        query = head_lanes(rows_ref, block, 0)
        lse = lse_ref[block, 0:1, :]

        def add(tile, total, mode):
            at = pl.multiple_of(tile * BK, BK)
            score = jnp.dot(keys_ref[pl.ds(at, BK), :], query, preferred_element_type=F32)
            if mode:
                score = masked(score, row, tile, block, mode == 2)
            probs = jnp.exp(score - lse).astype(BF)
            return total + jnp.dot(value_ref[tile], probs, preferred_element_type=F32)

        total = jnp.zeros((HD, LANES), F32)
        total = lax.fori_loop(begin, plain, lambda t, c: add(t, c, 1), total)
        total = lax.fori_loop(plain, last, lambda t, c: add(t, c, 0), total)
        total = add(last, total, 2).astype(BF)
        for h in range(GROUPS):
            out_ref[block, h * HD : (h + 1) * HD, :] = total[:, h * TOK : (h + 1) * TOK]
        return 0

    lax.fori_loop(0, NB, one_block, 0)


def outs(keys, values, rows, lse):
    return pl.pallas_call(
        outs_kernel,
        out_shape=jax.ShapeDtypeStruct((NB, GROUPS * HD, TOK), BF),
        scratch_shapes=[
            pltpu.VMEM((WIN * TOK, HD), BF),
            pltpu.VMEM((NB, TOK), jnp.int32),
            pltpu.VMEM((WIN * TOK // BK, HD, BK), BF),
        ],
        name="outs",
        compiler_params=params(),
    )(*keys, *values, rows, lse)


def weight_kernel(grad_ref, rows_ref, out_ref, left_ref, right_ref):
    part = GROUPS * HD
    for b in range(NB):
        at = slice(b * TOK, (b + 1) * TOK)
        left_ref[:, at] = rows_ref[b, 2 * part : 3 * part, :]
        for g in range(KVH):
            right_ref[g * HD : (g + 1) * HD, at] = grad_ref[g, b]
    out_ref[...] = dot(left_ref[...], right_ref[...], ((1,), (1,))).astype(BF)


def weight_part(value_grads, rows):
    return pl.pallas_call(
        weight_kernel,
        out_shape=jax.ShapeDtypeStruct((GROUPS * HD, KVD), BF),
        scratch_shapes=[pltpu.VMEM((GROUPS * HD, NB * TOK), BF), pltpu.VMEM((KVD, NB * TOK), BF)],
        name="weight_part",
        compiler_params=params(),
    )(value_grads, rows)


def shift(x, by):
    return lax.ppermute(x, "zh", [(z, z + by) for z in range(4) if 0 <= z + by < 4])


def exchange(x, axes):
    return lax.all_to_all(x, axes, split_axis=0, concat_axis=0, tiled=True)


def body(hidden, queries, key_states, upstream, value_weight, doc_ids):
    core = lax.axis_index("c")
    place = lax.axis_index(YC)
    half = KVD // 2

    key_own = exchange(pack_keys(key_states, doc_ids), YC)
    key_near, key_far = shift(key_own, 1), shift(key_own, 2)
    keys = (key_far, key_near, key_own)

    rows = exchange(pack_rows(queries, upstream, hidden), YC)

    my_half = lax.dynamic_slice_in_dim(value_weight, core * half, half, 1)
    mine = exchange(jnp.broadcast_to(my_half[None], (16, TOK, half)), ("x", "zl")).reshape(D, half)
    other = lax.ppermute(mine, "c", [(0, 1), (1, 0)])
    mine_v = dot(mine, hidden[0], ((0,), (1,))).astype(BF)
    other_v = dot(other, hidden[0], ((0,), (1,))).astype(BF)
    value = jnp.where(core == 0, jnp.concatenate([mine_v, other_v]), jnp.concatenate([other_v, mine_v]))
    value_own = exchange(value.reshape(KVH, HD, TOK), YC)

    grad_far, grad_near, grad_own, lse = grads(keys, rows)
    grad_own = grad_own + shift(grad_near, -1).astype(F32) + shift(grad_far, -2).astype(F32)
    mine_grad = grad_own.astype(BF)
    value_grads = exchange(jnp.broadcast_to(mine_grad[None], (KVH, NB, HD, TOK)), YC)

    value_near, value_far = shift(value_own, 1), shift(value_own, 2)
    out = outs(keys, (value_far, value_near, value_own), rows, lse)
    attn = exchange(out, YC).reshape(D, TOK).T.reshape(1, TOK, D)

    partial = weight_part(value_grads, rows).reshape(64, 4, KVD)
    grad_weight = exchange(partial, ("x", "zl", "zh")).astype(F32).sum(axis=0)

    here = lax.dynamic_index_in_dim(value_grads, place, 1, keepdims=False).reshape(2, half, TOK)
    here_mine = lax.dynamic_index_in_dim(here, core, 0, keepdims=False)
    here_other = lax.dynamic_index_in_dim(here, 1 - core, 0, keepdims=False)
    grad_hidden = dot(here_mine, mine, ((0,), (1,))) + dot(here_other, other, ((0,), (1,)))
    return attn, grad_hidden.astype(BF).reshape(1, TOK, D), grad_weight


def solution(mesh):
    fine = Mesh(np.asarray(mesh.devices).reshape(4, 4, 4, 4, 2), ("x", "zl", "zh", "y", "c"))
    dp, sp = ("x", "zl"), ("zh", "y", "c")
    return jax.shard_map(
        body,
        mesh=fine,
        in_specs=(P(dp, sp, None),) * 4 + (P(dp, None), P(dp, sp)),
        out_specs=(P(dp, sp, None), P(dp, sp, None), P(dp + sp, None)),
        check_vma=False,
    )
```

time: 940 us -> 254 us (0.27)
  the two profiles are of different devices: /device:TPU:2 before, /device:TPU:322 now
where the time goes in v1:
time: 254 us; the launch traced here: 253 us
  waiting for transfers between devices  104 us (41%)
  Pallas kernels  69.4 us (27%)
  starting transfers between devices  62 us (24%)
  local copies, waits for them, and re-layouts  8.54 us (3%)
  matrix products  5.17 us (2%)
    all_to_all x7, waiting for transfers between devices, exchange(): return lax.all_to_all(x, axes, split_axis=0, concat_axis=0, tiled=True)  65.7 us
    all_to_all x7, starting transfers between devices, exchange(): return lax.all_to_all(x, axes, split_axis=0, concat_axis=0, tiled=True)  47.4 us
    ppermute x6, waiting for transfers between devices, shift(): lax.ppermute(x, 'zh', [(z, z + by) for z in range(4) if 0 <= z + by < 4])  38.6 us
    pallas_call x1, Pallas kernels, grads(): pl.pallas_call(grads_kernel, out_shape=(jax.ShapeDtypeStruct(shape, BF),...  35.1 us
    pallas_call x1, Pallas kernels, outs(): pl.pallas_call(outs_kernel, out_shape=jax.ShapeDtypeStruct((NB, GROUPS *...  26.5 us
    ppermute x6, starting transfers between devices, shift(): lax.ppermute(x, 'zh', [(z, z + by) for z in range(4) if 0 <= z + by < 4])  12.6 us
    dot_general x4, matrix products, dot(): lax.dot_general(a, b, ((contract[0], contract[1]), ((), ())), preferred_e...  5.17 us
  transfers between devices with their start and end apart: 14, of which 10 were waited for; matrix products, arithmetic and copies ran while one was open for 5% of the time, Pallas kernels for 16%

profile of v1, /device:TPU:322, one launch (start us, length us, event | category | flops | bytes accessed | tf_op | source)
XLA Modules:
  0.0 252.6 jit_solution(15804248251489655225)
XLA Ops:
  0.6 0.0 copy-start
  0.6 1.7 pack_keys.1
  2.3 4.5 %all-to-all-start = ((bf16[8,80,128]{2,1,0:T(8,128)(2,1)}), bf16[8,80,128]{2,1,0:T(8,128)(2,1)S(1)}, u32[]{:S(2)}, u32[]{:S(2)}) async-start(bf16[8,80,128]{2,1,0:T(8,128)(2,1)} %pack_keys.1), calls=%async_computation | async-start | bytes 327680 | tf_op jit(solution)/shard_map/all_to_all | solution.py:278
  6.8 6.5 %all-to-all-done.own_ref = bf16[8,80,128]{2,1,0:T(8,128)(2,1)S(1)} async-done(((bf16[8,80,128]{2,1,0:T(8,128)(2,1)}), bf16[8,80,128]{2,1,0:T(8,128)(2,1)S(1)}, u32[]{:S(2)}, u32[]{:S(2)}) %all-to-all-start) | async-done | bytes 163872 | tf_op jit(solution)/shard_map/all_to_all | solution.py:278
  13.3 1.1 broadcast_in_dim.4
  14.4 7.1 %all-to-all-start.1 = ((bf16[16,128,256]{2,1,0:T(8,128)(2,1)}), bf16[16,128,256]{2,1,0:T(8,128)(2,1)S(1)}, u32[]{:S(2)}, u32[]{:S(2)}) async-start(bf16[16,128,256]{2,1,0:T(8,128)(2,1)} %broadcast_in_dim.4), calls=%async_computation.1 | async-start | bytes 2097152 | tf_op jit(solution)/shard_map/all_to_all | solution.py:278
  21.5 3.0 %pack_rows.1 = bf16[8,768,128]{2,1,0:T(8,128)(2,1)} custom-call(bf16[1,128,2048]{2,1,0:T(8,128)(2,1)} %query_ref.1, bf16[1,128,2048]{2,1,0:T(8,128)(2,1)} %up_ref.1, bf16[1,128,2048]{2,1,0:T(8,128)(2,1)} %hidden_ref.1), custom_call_target="tpu_custom_call" | custom-call | tf_op jit(solution)/shard_map/pack_rows/pallas_call | solution.py:70
  24.5 20.2 %all-to-all-done.1 = bf16[16,128,256]{2,1,0:T(8,128)(2,1)S(1)} async-done(((bf16[16,128,256]{2,1,0:T(8,128)(2,1)}), bf16[16,128,256]{2,1,0:T(8,128)(2,1)S(1)}, u32[]{:S(2)}, u32[]{:S(2)}) %all-to-all-start.1) | async-done | bytes 1048608 | tf_op jit(solution)/shard_map/all_to_all | solution.py:278
  44.8 3.6 %all-to-all-start.3 = ((bf16[8,768,128]{2,1,0:T(8,128)(2,1)}), bf16[8,768,128]{2,1,0:T(8,128)(2,1)S(1)}, u32[]{:S(2)}, u32[]{:S(2)}) async-start(bf16[8,768,128]{2,1,0:T(8,128)(2,1)} %pack_rows.1), calls=%async_computation.3 | async-start | bytes 3145728 | tf_op jit(solution)/shard_map/all_to_all | solution.py:278
  48.4 4.3 %collective-permute-start.1 = (bf16[8,80,128]{2,1,0:T(8,128)(2,1)S(1)}, bf16[8,80,128]{2,1,0:T(8,128)(2,1)S(1)}, u32[]{:S(2)}, u32[]{:S(2)}) collective-permute-start(bf16[8,80,128]{2,1,0:T(8,128)(2,1)S(1)} %all-to-all-done.own_ref), channel_id=1, source_target_pairs={{0,8},{8,16},{16,24},{1,9},{9,17},{17,25},{2,10},{10,18},{18,26},{... | collective-permute-start | bytes 491528 | tf_op jit(solution)/shard_map/ppermute | solution.py:274
  52.7 1.3 collective-permute-start
  54.0 2.0 collective-permute-start.2
  56.0 15.7 %collective-permute-done.1.near_ref = bf16[8,80,128]{2,1,0:T(8,128)(2,1)S(1)} collective-permute-done((bf16[8,80,128]{2,1,0:T(8,128)(2,1)S(1)}, bf16[8,80,128]{2,1,0:T(8,128)(2,1)S(1)}, u32[]{:S(2)}, u32[]{:S(2)}) %collective-permute-start.1) | collective-permute-done | bytes 163872 | tf_op jit(solution)/shard_map/ppermute | solution.py:274
  71.7 4.2 %collective-permute-done.far_ref = bf16[8,80,128]{2,1,0:T(8,128)(2,1)S(1)} collective-permute-done((bf16[8,80,128]{2,1,0:T(8,128)(2,1)S(1)}, bf16[8,80,128]{2,1,0:T(8,128)(2,1)S(1)}, u32[]{:S(2)}, u32[]{:S(2)}) %collective-permute-start) | collective-permute-done | bytes 163872 | tf_op jit(solution)/shard_map/ppermute | solution.py:274
  75.9 0.6 copy-done.6
  76.5 1.2 copy-done.1
  77.7 35.1 %grads.1 = (bf16[8,64,128]{2,1,0:T(8,128)(2,1)}, bf16[8,64,128]{2,1,0:T(8,128)(2,1)}, f32[8,64,128]{2,1,0:T(8,128)}, f32[8,8,512]{2,1,0:T(8,128)}) custom-call(bf16[8,80,128]{2,1,0:T(8,128)(2,1)} %copy-done.6, bf16[8,80,128]{2,1,0:T(8,128)(2,1)} %copy-done.5, bf16[8,80,128]{2,1,0:T(8,128)(2,1)} %copy-done.4, bf16[8,768,128]{2,1,0:T(8,128)(2,1)} %copy-done.1), custom_call_target="tpu_custom_call" | custom-call | tf_op jit(solution)/shard_map/grads/pallas_call | solution.py:184
  112.8 1.9 collective-permute-start.5
  114.7 1.3 collective-permute-start.6
  116.0 7.9 %collective-permute-done.5 = bf16[8,64,128]{2,1,0:T(8,128)(2,1)S(1)} collective-permute-done((bf16[8,64,128]{2,1,0:T(8,128)(2,1)}, bf16[8,64,128]{2,1,0:T(8,128)(2,1)S(1)}, u32[]{:S(2)}, u32[]{:S(2)}) %collective-permute-start.5) | collective-permute-done | bytes 131104 | tf_op jit(solution)/shard_map/ppermute | solution.py:274
  124.0 0.0 collective-permute-done.6
  124.0 1.0 add_convert_fusion
  125.0 0.0 copy-start.3
  125.0 1.2 broadcast_in_dim.5
  126.2 4.5 %all-to-all-start.5 = ((bf16[8,8,64,128]{3,2,1,0:T(8,128)(2,1)}), bf16[8,8,64,128]{3,2,1,0:T(8,128)(2,1)S(1)}, u32[]{:S(2)}, u32[]{:S(2)}) async-start(bf16[8,8,64,128]{3,2,1,0:T(8,128)(2,1)} %broadcast_in_dim.5), calls=%async_computation.5 | async-start | bytes 2097152 | tf_op jit(solution)/shard_map/all_to_all | solution.py:278
  130.7 0.5 convolution_convert_fusion.1
  131.2 1.7 convolution_convert_fusion
  132.9 0.7 maximum_select_fusion
  133.6 13.1 %all-to-all-done.5.grad_ref = bf16[8,8,64,128]{3,2,1,0:T(8,128)(2,1)S(1)} async-done(((bf16[8,8,64,128]{3,2,1,0:T(8,128)(2,1)}), bf16[8,8,64,128]{3,2,1,0:T(8,128)(2,1)S(1)}, u32[]{:S(2)}, u32[]{:S(2)}) %all-to-all-start.5) | async-done | bytes 1048608 | tf_op jit(solution)/shard_map/all_to_all | solution.py:278
  146.7 3.4 %all-to-all-start.2 = ((bf16[8,64,128]{2,1,0:T(8,128)(2,1)}), bf16[8,64,128]{2,1,0:T(8,128)(2,1)S(1)}, u32[]{:S(2)}, u32[]{:S(2)}) async-start(bf16[8,64,128]{2,1,0:T(8,128)(2,1)} %bitcast.2), calls=%async_computation.2 | async-start | bytes 262144 | tf_op jit(solution)/shard_map/all_to_all | solution.py:278
  150.1 3.0 %weight_part.1 = bf16[256,512]{1,0:T(8,128)(2,1)} custom-call(bf16[8,8,64,128]{3,2,1,0:T(8,128)(2,1)} %copy-done.2, bf16[8,768,128]{2,1,0:T(8,128)(2,1)} %copy-done.1), custom_call_target="tpu_custom_call" | custom-call | tf_op jit(solution)/shard_map/weight_part/pallas_call | solution.py:264
  153.1 1.7 reshape.37
  154.8 1.3 all-to-all-done.2.vown_ref
  156.1 20.6 %all-to-all-start.6 = ((bf16[64,4,512]{2,1,0:T(4,128)(2,1)}), bf16[64,4,512]{2,1,0:T(4,128)(2,1)S(1)}, u32[]{:S(2)}, u32[]{:S(2)}) async-start(bf16[64,4,512]{2,1,0:T(4,128)(2,1)} %reshape.37), calls=%async_computation.6 | async-start | bytes 524288 | tf_op jit(solution)/shard_map/all_to_all | solution.py:278
  176.8 0.9 constant_dynamic-slice_fusion
  177.7 2.5 collective-permute-start.4
  180.2 1.3 collective-permute-start.3
  181.5 17.3 %all-to-all-done.6 = bf16[64,4,512]{2,1,0:T(4,128)(2,1)S(1)} async-done(((bf16[64,4,512]{2,1,0:T(4,128)(2,1)}), bf16[64,4,512]{2,1,0:T(4,128)(2,1)S(1)}, u32[]{:S(2)}, u32[]{:S(2)}) %all-to-all-start.6) | async-done | bytes 262176 | tf_op jit(solution)/shard_map/all_to_all | solution.py:278
  198.7 0.7 convert_reduce_fusion
  199.5 10.7 %collective-permute-done.4.vnear_ref = bf16[8,64,128]{2,1,0:T(8,128)(2,1)S(1)} collective-permute-done((bf16[8,64,128]{2,1,0:T(8,128)(2,1)S(1)}, bf16[8,64,128]{2,1,0:T(8,128)(2,1)S(1)}, u32[]{:S(2)}, u32[]{:S(2)}) %collective-permute-start.4) | collective-permute-done | bytes 131104 | tf_op jit(solution)/shard_map/ppermute | solution.py:274
  210.2 0.6 copy-done.8
  210.9 0.1 copy-done.9
  210.9 26.5 %outs.1 = bf16[8,256,128]{2,1,0:T(8,128)(2,1)} custom-call(bf16[8,80,128]{2,1,0:T(8,128)(2,1)} %copy-done.6, bf16[8,80,128]{2,1,0:T(8,128)(2,1)} %copy-done.5, bf16[8,80,128]{2,1,0:T(8,128)(2,1)} %copy-done.4, bf16[8,64,128]{2,1,0:T(8,128)(2,1)} %copy-done.9, bf16[8,64,128]{2,1,0:T(8,128)(2,1)} %copy-done.8, bf16[8,64,128]{2,1,0:T(8,128)(2,1)} %copy-done.7, ...), custom_call_target="tpu_custom_call" | custom-call | tf_op jit(solution)/shard_map/outs/pallas_call | solution.py:240
  237.5 3.8 %all-to-all-start.4 = ((bf16[8,256,128]{2,1,0:T(8,128)(2,1)}), bf16[8,256,128]{2,1,0:T(8,128)(2,1)S(1)}, u32[]{:S(2)}, u32[]{:S(2)}) async-start(bf16[8,256,128]{2,1,0:T(8,128)(2,1)} %outs.1), calls=%async_computation.4 | async-start | bytes 1048576 | tf_op jit(solution)/shard_map/all_to_all | solution.py:278
  241.2 0.5 fusion.5
  241.7 2.5 fusion.1
  244.2 7.4 %all-to-all-done.4 = bf16[8,256,128]{2,1,0:T(8,128)(2,1)S(1)} async-done(((bf16[8,256,128]{2,1,0:T(8,128)(2,1)}), bf16[8,256,128]{2,1,0:T(8,128)(2,1)S(1)}, u32[]{:S(2)}, u32[]{:S(2)}) %all-to-all-start.4) | async-done | bytes 524320 | tf_op jit(solution)/shard_map/all_to_all | solution.py:278
  251.6 1.0 copy.9
  (18 shorter events, 0.0 us)
Async XLA Ops:
  0.6 6.2 %copy-start = (bf16[128,512]{1,0:T(8,128)(2,1)S(1)}, bf16[128,512]{1,0:T(8,128)(2,1)}, u32[]{:S(2)}) copy-start(bf16[128,512]{1,0:T(8,128)(2,1)} %param.10) | copy-start | bytes 393220
  2.3 11.0 %all-to-all-start = ((bf16[8,80,128]{2,1,0:T(8,128)(2,1)}), bf16[8,80,128]{2,1,0:T(8,128)(2,1)S(1)}, u32[]{:S(2)}, u32[]{:S(2)}) async-start(bf16[8,80,128]{2,1,0:T(8,128)(2,1)} %pack_keys.1), calls=%async_computation | async-start | bytes 327680 | tf_op jit(solution)/shard_map/all_to_all | solution.py:278
  13.3 39.4 %copy-start.4 = (bf16[8,80,128]{2,1,0:T(8,128)(2,1)}, bf16[8,80,128]{2,1,0:T(8,128)(2,1)S(1)}, u32[]{:S(2)}) copy-start(bf16[8,80,128]{2,1,0:T(8,128)(2,1)S(1)} %all-to-all-done.own_ref) | copy-start | bytes 491524
  14.4 30.4 %all-to-all-start.1 = ((bf16[16,128,256]{2,1,0:T(8,128)(2,1)}), bf16[16,128,256]{2,1,0:T(8,128)(2,1)S(1)}, u32[]{:S(2)}, u32[]{:S(2)}) async-start(bf16[16,128,256]{2,1,0:T(8,128)(2,1)} %broadcast_in_dim.4), calls=%async_computation.1 | async-start | bytes 2097152 | tf_op jit(solution)/shard_map/all_to_all | solution.py:278
  44.8 31.1 %all-to-all-start.3 = ((bf16[8,768,128]{2,1,0:T(8,128)(2,1)}), bf16[8,768,128]{2,1,0:T(8,128)(2,1)S(1)}, u32[]{:S(2)}, u32[]{:S(2)}) async-start(bf16[8,768,128]{2,1,0:T(8,128)(2,1)} %pack_rows.1), calls=%async_computation.3 | async-start | bytes 3145728 | tf_op jit(solution)/shard_map/all_to_all | solution.py:278
  48.4 23.4 %collective-permute-start.1 = (bf16[8,80,128]{2,1,0:T(8,128)(2,1)S(1)}, bf16[8,80,128]{2,1,0:T(8,128)(2,1)S(1)}, u32[]{:S(2)}, u32[]{:S(2)}) collective-permute-start(bf16[8,80,128]{2,1,0:T(8,128)(2,1)S(1)} %all-to-all-done.own_ref), channel_id=1, source_target_pairs={{0,8},{8,16},{16,24},{1,9},{9,17},{17,25},{2,10},{10,18},{18,26},{... | collective-permute-start | bytes 491528 | tf_op jit(solution)/shard_map/ppermute | solution.py:274
  52.7 23.2 %collective-permute-start = (bf16[8,80,128]{2,1,0:T(8,128)(2,1)S(1)}, bf16[8,80,128]{2,1,0:T(8,128)(2,1)S(1)}, u32[]{:S(2)}, u32[]{:S(2)}) collective-permute-start(bf16[8,80,128]{2,1,0:T(8,128)(2,1)S(1)} %all-to-all-done.own_ref), channel_id=1, source_target_pairs={{0,16},{8,24},{1,17},{9,25},{2,18},{10,26},{3,19},{11,27},{4,20},{... | collective-permute-start | bytes 491528 | tf_op jit(solution)/shard_map/ppermute | solution.py:274
  54.0 77.2 %collective-permute-start.2 = (bf16[2048,256]{1,0:T(8,128)(2,1)S(1)}, bf16[2048,256]{1,0:T(8,128)(2,1)}, u32[]{:S(2)}, u32[]{:S(2)}) collective-permute-start(bf16[2048,256]{1,0:T(8,128)(2,1)S(1)} %bitcast.24), channel_id=1, source_target_pairs={{0,1},{1,0},{2,3},{3,2},{4,5},{5,4},{6,7},{7,6},{8,9},{9,8},{10,11... | collective-permute-start | bytes 3145736 | tf_op jit(solution)/shard_map/ppermute | solution.py:294
  71.7 4.2 %copy-start.5 = (bf16[8,80,128]{2,1,0:T(8,128)(2,1)}, bf16[8,80,128]{2,1,0:T(8,128)(2,1)S(1)}, u32[]{:S(2)}) copy-start(bf16[8,80,128]{2,1,0:T(8,128)(2,1)S(1)} %collective-permute-done.1.near_ref) | copy-start | bytes 491524
  75.9 0.7 copy-start.6
  76.5 1.2 copy-start.1
  112.8 11.1 %collective-permute-start.5 = (bf16[8,64,128]{2,1,0:T(8,128)(2,1)}, bf16[8,64,128]{2,1,0:T(8,128)(2,1)S(1)}, u32[]{:S(2)}, u32[]{:S(2)}) collective-permute-start(bf16[8,64,128]{2,1,0:T(8,128)(2,1)} %get-tuple-element.9), channel_id=1, source_target_pairs={{8,0},{16,8},{24,16},{9,1},{17,9},{25,17},{10,2},{18,10},{26,18},{... | collective-permute-start | bytes 393224 | tf_op jit(solution)/shard_map/ppermute | solution.py:274
  114.7 9.2 %collective-permute-start.6 = (bf16[8,64,128]{2,1,0:T(8,128)(2,1)}, bf16[8,64,128]{2,1,0:T(8,128)(2,1)S(1)}, u32[]{:S(2)}, u32[]{:S(2)}) collective-permute-start(bf16[8,64,128]{2,1,0:T(8,128)(2,1)} %get-tuple-element.10), channel_id=1, source_target_pairs={{16,0},{24,8},{17,1},{25,9},{18,2},{26,10},{19,3},{27,11},{20,4},{... | collective-permute-start | bytes 393224 | tf_op jit(solution)/shard_map/ppermute | solution.py:274
  125.0 5.7 %copy-start.3 = (bf16[1,128,2048]{2,1,0:T(8,128)(2,1)S(1)}, bf16[1,128,2048]{2,1,0:T(8,128)(2,1)}, u32[]{:S(2)}) copy-start(bf16[1,128,2048]{2,1,0:T(8,128)(2,1)} %hidden_ref.1) | copy-start | bytes 1572868
  126.2 20.5 %all-to-all-start.5 = ((bf16[8,8,64,128]{3,2,1,0:T(8,128)(2,1)}), bf16[8,8,64,128]{3,2,1,0:T(8,128)(2,1)S(1)}, u32[]{:S(2)}, u32[]{:S(2)}) async-start(bf16[8,8,64,128]{3,2,1,0:T(8,128)(2,1)} %broadcast_in_dim.5), calls=%async_computation.5 | async-start | bytes 2097152 | tf_op jit(solution)/shard_map/all_to_all | solution.py:278
  146.7 3.4 %copy-start.2 = (bf16[8,8,64,128]{3,2,1,0:T(8,128)(2,1)}, bf16[8,8,64,128]{3,2,1,0:T(8,128)(2,1)S(1)}, u32[]{:S(2)}) copy-start(bf16[8,8,64,128]{3,2,1,0:T(8,128)(2,1)S(1)} %all-to-all-done.5.grad_ref) | copy-start | bytes 3145732
  146.7 9.4 %all-to-all-start.2 = ((bf16[8,64,128]{2,1,0:T(8,128)(2,1)}), bf16[8,64,128]{2,1,0:T(8,128)(2,1)S(1)}, u32[]{:S(2)}, u32[]{:S(2)}) async-start(bf16[8,64,128]{2,1,0:T(8,128)(2,1)} %bitcast.2), calls=%async_computation.2 | async-start | bytes 262144 | tf_op jit(solution)/shard_map/all_to_all | solution.py:278
  156.1 54.1 %copy-start.7 = (bf16[8,64,128]{2,1,0:T(8,128)(2,1)}, bf16[8,64,128]{2,1,0:T(8,128)(2,1)S(1)}, u32[]{:S(2)}) copy-start(bf16[8,64,128]{2,1,0:T(8,128)(2,1)S(1)} %all-to-all-done.2.vown_ref) | copy-start | bytes 393220
  156.1 42.6 %all-to-all-start.6 = ((bf16[64,4,512]{2,1,0:T(4,128)(2,1)}), bf16[64,4,512]{2,1,0:T(4,128)(2,1)S(1)}, u32[]{:S(2)}, u32[]{:S(2)}) async-start(bf16[64,4,512]{2,1,0:T(4,128)(2,1)} %reshape.37), calls=%async_computation.6 | async-start | bytes 524288 | tf_op jit(solution)/shard_map/all_to_all | solution.py:278
  177.7 32.5 %collective-permute-start.4 = (bf16[8,64,128]{2,1,0:T(8,128)(2,1)S(1)}, bf16[8,64,128]{2,1,0:T(8,128)(2,1)S(1)}, u32[]{:S(2)}, u32[]{:S(2)}) collective-permute-start(bf16[8,64,128]{2,1,0:T(8,128)(2,1)S(1)} %all-to-all-done.2.vown_ref), channel_id=1, source_target_pairs={{0,8},{8,16},{16,24},{1,9},{9,17},{17,25},{2,10},{10,18},{18,26},{... | collective-permute-start | bytes 393224 | tf_op jit(solution)/shard_map/ppermute | solution.py:274
  180.2 30.1 %collective-permute-start.3 = (bf16[8,64,128]{2,1,0:T(8,128)(2,1)S(1)}, bf16[8,64,128]{2,1,0:T(8,128)(2,1)S(1)}, u32[]{:S(2)}, u32[]{:S(2)}) collective-permute-start(bf16[8,64,128]{2,1,0:T(8,128)(2,1)S(1)} %all-to-all-done.2.vown_ref), channel_id=1, source_target_pairs={{0,16},{8,24},{1,17},{9,25},{2,18},{10,26},{3,19},{11,27},{4,20},{... | collective-permute-start | bytes 393224 | tf_op jit(solution)/shard_map/ppermute | solution.py:274
  210.2 0.6 copy-start.8
  210.2 0.7 copy-start.9
  237.5 14.1 %all-to-all-start.4 = ((bf16[8,256,128]{2,1,0:T(8,128)(2,1)}), bf16[8,256,128]{2,1,0:T(8,128)(2,1)S(1)}, u32[]{:S(2)}, u32[]{:S(2)}) async-start(bf16[8,256,128]{2,1,0:T(8,128)(2,1)} %outs.1), calls=%async_computation.4 | async-start | bytes 1048576 | tf_op jit(solution)/shard_map/all_to_all | solution.py:278
